TPU v7x, 768 devices: a whole 4x8x12 slice. The times are simulated.
768 devices in a mesh: pipe: 24 (over z, core), expert: 32 (over x, y).
Axes of the slice: x: 4, y: 8, z: 12, core: 2. Of those that a mesh axis runs over, the one named last changes fastest.
Arguments:
- tokens: bfloat16 [24, 4096, 3584], P('pipe', 'expert'), may hold values from -6 to 6
- routing: int32 [24, 4096, 1], P('pipe', 'expert'), may hold values from 0 to 3; in each aligned block of 128 rows (0 to 127, 128 to 255, ..., all dimensions but the last counted through in order) at most 34 rows name the same one
- scores: float32 [24, 4096, 1], P('pipe', 'expert'), may hold values from 0.2 to 1
- w_gate: bfloat16 [24, 32, 896, 512], P('pipe', 'expert'), may hold values from -0.09375 to 0.09375
- w_up: bfloat16 [24, 32, 896, 512], P('pipe', 'expert'), may hold values from -0.09375 to 0.09375
- w_down: bfloat16 [24, 32, 1024, 448], P('pipe', 'expert'), may hold values from -0.1875 to 0.1875
Outputs:
- passed: bfloat16 [24, 4096, 3584], P('pipe', 'expert')
Inputs may be any that keep to these rules, and one draw needn't show every extreme that they name: `routing`: within one device's 128 tokens no expert is chosen more than 34 times, a bound that some block reaches.
All inputs are finite; a program needn't handle non-finite values.
Results may differ from a plain program's by a relative error of at most 0.0035.
Values may be sent and summed in bfloat16 or wider, within the bound.
A program may use at most 32 MiB of HBM per device.

v0:
```python
import jax
import jax.numpy as jnp
from jax import lax
from jax.sharding import PartitionSpec as P


def from_partner(block, axis, distance):
    count = lax.axis_size(axis)
    route = []
    for low in range(count):
        high = low | 1 << distance
        if high != low and high < count:
            route += [(low, high), (high, low)]
    return lax.ppermute(block, axis, route)


def from_behind(x, axis, by):
    size = lax.axis_size(axis)
    pairs = [(i, i + by) for i in range(size) if 0 <= i + by < size]
    return lax.ppermute(x, axis, pairs)


def route_matrix(choice_col, experts_here, capacity):
    matches = (choice_col == jnp.arange(experts_here, dtype=jnp.int32)[None, :]).astype(jnp.int32)
    slot_index = jnp.sum(jnp.cumsum(matches, axis=0) * matches, axis=1) - 1
    target = choice_col[:, 0] * capacity + slot_index
    return (
        jnp.arange(experts_here * capacity, dtype=jnp.int32)[:, None] == target[None, :]
    ).astype(jnp.bfloat16)


def pack_rows(selector, x_rows, experts_here, capacity):
    buffer = jnp.dot(selector, x_rows, preferred_element_type=jnp.float32).astype(jnp.bfloat16)
    quarter = x_rows.shape[1] // 4
    buffer = buffer.reshape(experts_here, capacity, 4, quarter).transpose(0, 2, 1, 3)
    buffer = jnp.broadcast_to(buffer[:, :, None], (experts_here, 4, 2, capacity, quarter))
    return buffer.reshape(experts_here * 8, capacity, quarter)


def group_expert(outgoing, gate_w, up_w, down_w, position):
    arrived = lax.all_to_all(outgoing, "expert", split_axis=0, concat_axis=0, tiled=True)
    row_count = arrived.shape[0] * arrived.shape[1]
    row_block = arrived.reshape(row_count, arrived.shape[2])
    current = jnp.stack(
        [
            jnp.dot(row_block, gate_w, preferred_element_type=jnp.float32),
            jnp.dot(row_block, up_w, preferred_element_type=jnp.float32),
        ]
    )
    reduce_bits = (2, 1)
    gather_bits = (1, 2, 0)
    for bit_index in reduce_bits:
        chosen = position >> bit_index & 1
        half_cols = current.shape[2] // 2
        kept_part = lax.dynamic_slice_in_dim(current, chosen * half_cols, half_cols, 2)
        sent_part = lax.dynamic_slice_in_dim(current, (1 - chosen) * half_cols, half_cols, 2)
        current = kept_part + from_partner(sent_part, "expert", bit_index)
    hidden = (jax.nn.silu(current[0]) * current[1]).astype(jnp.bfloat16)
    for bit_index in gather_bits:
        partner = from_partner(hidden, "expert", bit_index)
        chosen = position >> bit_index & 1
        hidden = jnp.where(
            chosen == 0,
            jnp.concatenate([hidden, partner], axis=1),
            jnp.concatenate([partner, hidden], axis=1),
        )
    result = jnp.dot(hidden, down_w, preferred_element_type=jnp.float32).astype(jnp.bfloat16)
    result = result.reshape(arrived.shape[0], arrived.shape[1], result.shape[1])
    return lax.all_to_all(result, "expert", split_axis=0, concat_axis=0, tiled=True)


def unpack_rows(returned, selector, experts_here, capacity):
    eighth = returned.shape[2]
    ordered = returned.reshape(experts_here, 8, capacity, eighth).transpose(0, 2, 1, 3)
    ordered = ordered.reshape(experts_here * capacity, 8 * eighth)
    return lax.dot_general(
        selector, ordered, (((0,), (0,)), ((), ())), preferred_element_type=jnp.float32
    )


def body(tokens, routing, scores, w_gate, w_up, w_down):
    groups = lax.axis_size("expert")
    experts_here = groups // 8
    tok_count = tokens.shape[1]
    capacity = min(tok_count, 17 * tok_count // (16 * experts_here))
    position = lax.axis_index("expert")
    parity = lax.axis_index("pipe") % 2
    selector = route_matrix(routing[0], experts_here, capacity)
    outgoing = pack_rows(selector, tokens[0], experts_here, capacity)
    returned = group_expert(outgoing, w_gate[0, 0], w_up[0, 0], w_down[0, 0], position)
    expert_out = unpack_rows(returned, selector, experts_here, capacity)
    mixed_rows = (tokens[0].astype(jnp.float32) + scores[0] * expert_out).astype(jnp.bfloat16)
    below = from_behind(mixed_rows, "pipe", 1)
    above = from_behind(mixed_rows, "pipe", -1)
    return jnp.where(parity == 0, above, below)[None]


def solution(mesh):
    return jax.shard_map(
        body,
        mesh=mesh,
        in_specs=(
            P("pipe", "expert", None),
            P("pipe", "expert", None),
            P("pipe", "expert", None),
            P("pipe", "expert", None, None),
            P("pipe", "expert", None, None),
            P("pipe", "expert", None, None),
        ),
        out_specs=P("pipe", "expert", None),
        check_vma=False,
    )
```

profile of v0, /device:TPU:1, one launch (start us, length us, event | category | flops | bytes accessed | tf_op | source)
XLA Modules:
  0.0 382.6 jit_solution(11927376481944321573)
XLA Ops:
  1.0 0.8 select_reduce_fusion
  2.5 1.6 convolution_convert_fusion
  4.5 1.6 broadcast_in_dim.4
  6.0 10.5 %all-to-all-start = ((bf16[32,34,896]{2,1,0:T(8,128)(2,1)}), bf16[32,34,896]{2,1,0:T(8,128)(2,1)S(1)}, u32[]{:S(2)}, u32[]{:S(2)}) async-start(bf16[32,34,896]{2,1,0:T(8,128)(2,1)} %bitcast.43), calls=%async_computation | async-start | bytes 4587520 | tf_op jit(solution)/shard_map/all_to_all | solution.py:41
  16.5 50.4 %all-to-all-done = bf16[32,34,896]{2,1,0:T(8,128)(2,1)S(1)} async-done(((bf16[32,34,896]{2,1,0:T(8,128)(2,1)}), bf16[32,34,896]{2,1,0:T(8,128)(2,1)S(1)}, u32[]{:S(2)}, u32[]{:S(2)}) %all-to-all-start) | async-done | bytes 1949728 | tf_op jit(solution)/shard_map/all_to_all | solution.py:41
  66.9 2.1 reshape.32
  69.0 3.0 convolution_bitcast_fusion
  72.0 1.3 convolution_bitcast_fusion.1
  73.7 1.1 copy-done.2
  74.8 4.6 %collective-permute-start = (f32[2,1088,256]{2,1,0:T(8,128)S(1)}, f32[2,1088,256]{2,1,0:T(8,128)}, u32[]{:S(2)}, u32[]{:S(2)}) collective-permute-start(f32[2,1088,256]{2,1,0:T(8,128)S(1)} %fusion.2), channel_id=1, source_target_pairs={{0,4},{4,0},{1,5},{5,1},{2,6},{6,2},{3,7},{7,3},{8,12},{12,8},{9,1... | collective-permute-start | bytes 6684680 | tf_op jit(solution)/shard_map/ppermute | solution.py:14
  79.4 60.4 %collective-permute-done = f32[2,1088,256]{2,1,0:T(8,128)} collective-permute-done((f32[2,1088,256]{2,1,0:T(8,128)S(1)}, f32[2,1088,256]{2,1,0:T(8,128)}, u32[]{:S(2)}, u32[]{:S(2)}) %collective-permute-start) | collective-permute-done | bytes 2228256 | tf_op jit(solution)/shard_map/ppermute | solution.py:14
  139.8 2.5 fusion.4
  142.3 1.1 constant_dynamic-slice_fusion
  143.4 40.8 %collective-permute-start.1 = (f32[2,1088,128]{2,1,0:T(8,128)}, f32[2,1088,128]{2,1,0:T(8,128)}, u32[]{:S(2)}, u32[]{:S(2)}) collective-permute-start(f32[2,1088,128]{2,1,0:T(8,128)} %constant_dynamic-slice_fusion), channel_id=1, source_target_pairs={{0,2},{2,0},{1,3},{3,1},{4,6},{6,4},{5,7},{7,5},{8,10},{10,8},{9,1... | collective-permute-start | bytes 3342344 | tf_op jit(solution)/shard_map/ppermute | solution.py:14
  184.2 48.7 %collective-permute-done.1 = f32[2,1088,128]{2,1,0:T(8,128)} collective-permute-done((f32[2,1088,128]{2,1,0:T(8,128)}, f32[2,1088,128]{2,1,0:T(8,128)}, u32[]{:S(2)}, u32[]{:S(2)}) %collective-permute-start.1) | collective-permute-done | bytes 1114144 | tf_op jit(solution)/shard_map/ppermute | solution.py:14
  232.9 1.4 dynamic-slice_add_fusion
  234.5 1.9 collective-permute-start.2
  236.4 14.0 %collective-permute-done.2 = bf16[1088,128]{1,0:T(8,128)(2,1)S(1)} collective-permute-done((bf16[1088,128]{1,0:T(8,128)(2,1)S(1)}, bf16[1088,128]{1,0:T(8,128)(2,1)S(1)}, u32[]{:S(2)}, u32[]{:S(2)}) %collective-permute-start.2) | collective-permute-done | bytes 278560 | tf_op jit(solution)/shard_map/ppermute | solution.py:14
  250.6 1.9 collective-permute-start.3
  252.6 26.8 %collective-permute-done.3 = bf16[1088,256]{1,0:T(8,128)(2,1)S(1)} collective-permute-done((bf16[1088,256]{1,0:T(8,128)(2,1)S(1)}, bf16[1088,256]{1,0:T(8,128)(2,1)S(1)}, u32[]{:S(2)}, u32[]{:S(2)}) %collective-permute-start.3) | collective-permute-done | bytes 557088 | tf_op jit(solution)/shard_map/ppermute | solution.py:14
  279.6 1.9 collective-permute-start.4
  281.5 24.7 %collective-permute-done.4 = bf16[1088,512]{1,0:T(8,128)(2,1)} collective-permute-done((bf16[1088,512]{1,0:T(8,128)(2,1)S(1)}, bf16[1088,512]{1,0:T(8,128)(2,1)}, u32[]{:S(2)}, u32[]{:S(2)}) %collective-permute-start.4) | collective-permute-done | bytes 1114144 | tf_op jit(solution)/shard_map/ppermute | solution.py:14
  306.2 4.3 %convolution_convert_fusion.1 = bf16[1088,448]{0,1:T(8,128)(2,1)} fusion(bf16[1088,512]{1,0:T(8,128)(2,1)} %collective-permute-done.4, bf16[1088,512]{1,0:T(8,128)(2,1)S(1)} %maximum_select_fusion.2, pred[]{:T(512)S(6)} %eq.47, bf16[1,1,1024,448]{2,3,1,0:T(8,128)(2,1)} %param.11), kind=kOutput, calls=%fused_computation.10 | convolution fusion | flops 1008758784 | bytes 4120577 | tf_op jit(solution)/shard_map/dot_general | solution.py:67
  310.5 1.8 copy.9
  312.7 42.0 %all_to_all.10 = bf16[32,34,448]{2,1,0:T(8,128)(2,1)S(1)} all-to-all(bf16[32,34,448]{2,1,0:T(8,128)(2,1)S(1)} %reshape.33), channel_id=1, replica_groups=mesh['pipe'=24,'expert'=32] {'expert'}, dimensions={0} | all-to-all | bytes 1949696 | tf_op jit(solution)/shard_map/all_to_all | solution.py:69
  355.0 1.2 reshape.35
  356.3 1.7 fusion.1
  358.0 6.9 %collective-permute-start.5 = (bf16[128,3584]{1,0:T(8,128)(2,1)S(1)}, bf16[128,3584]{1,0:T(8,128)(2,1)S(1)}, u32[]{:S(2)}, u32[]{:S(2)}) collective-permute-start(bf16[128,3584]{1,0:T(8,128)(2,1)S(1)} %fusion.1), channel_id=1, source_target_pairs={{32,0},{64,32},{96,64},{128,96},{160,128},{192,160},{224,192},{256... | collective-permute-start | bytes 2752520 | tf_op jit(solution)/shard_map/ppermute | solution.py:20
  364.9 5.2 %collective-permute-start.6 = (bf16[128,3584]{1,0:T(8,128)(2,1)S(1)}, bf16[128,3584]{1,0:T(8,128)(2,1)}, u32[]{:S(2)}, u32[]{:S(2)}) collective-permute-start(bf16[128,3584]{1,0:T(8,128)(2,1)S(1)} %fusion.1), channel_id=1, source_target_pairs={{0,32},{32,64},{64,96},{96,128},{128,160},{160,192},{192,224},{224... | collective-permute-start | bytes 2752520 | tf_op jit(solution)/shard_map/ppermute | solution.py:20
  370.1 9.1 %collective-permute-done.5 = bf16[128,3584]{1,0:T(8,128)(2,1)S(1)} collective-permute-done((bf16[128,3584]{1,0:T(8,128)(2,1)S(1)}, bf16[128,3584]{1,0:T(8,128)(2,1)S(1)}, u32[]{:S(2)}, u32[]{:S(2)}) %collective-permute-start.5) | collective-permute-done | bytes 917536 | tf_op jit(solution)/shard_map/ppermute | solution.py:20
  379.2 1.2 collective-permute-done.6
  380.4 2.2 select_bitcast_fusion
  (22 shorter events, 3.7 us)
Async XLA Ops:
  0.0 69.0 %copy-start = (bf16[1,1,896,512]{3,2,1,0:T(8,128)(2,1)S(1)}, bf16[1,1,896,512]{3,2,1,0:T(8,128)(2,1)}, u32[]{:S(2)}) copy-start(bf16[1,1,896,512]{3,2,1,0:T(8,128)(2,1)} %param.10) | copy-start | bytes 2752516
  6.0 60.9 %all-to-all-start = ((bf16[32,34,896]{2,1,0:T(8,128)(2,1)}), bf16[32,34,896]{2,1,0:T(8,128)(2,1)S(1)}, u32[]{:S(2)}, u32[]{:S(2)}) async-start(bf16[32,34,896]{2,1,0:T(8,128)(2,1)} %bitcast.43), calls=%async_computation | async-start | bytes 4587520 | tf_op jit(solution)/shard_map/all_to_all | solution.py:41
  69.0 3.0 copy-start.3
  69.0 3.0 copy-start.5
  72.0 1.4 copy-start.1
  73.4 1.3 copy-start.2
  74.8 65.0 %collective-permute-start = (f32[2,1088,256]{2,1,0:T(8,128)S(1)}, f32[2,1088,256]{2,1,0:T(8,128)}, u32[]{:S(2)}, u32[]{:S(2)}) collective-permute-start(f32[2,1088,256]{2,1,0:T(8,128)S(1)} %fusion.2), channel_id=1, source_target_pairs={{0,4},{4,0},{1,5},{5,1},{2,6},{6,2},{3,7},{7,3},{8,12},{12,8},{9,1... | collective-permute-start | bytes 6684680 | tf_op jit(solution)/shard_map/ppermute | solution.py:14
  143.4 89.5 %collective-permute-start.1 = (f32[2,1088,128]{2,1,0:T(8,128)}, f32[2,1088,128]{2,1,0:T(8,128)}, u32[]{:S(2)}, u32[]{:S(2)}) collective-permute-start(f32[2,1088,128]{2,1,0:T(8,128)} %constant_dynamic-slice_fusion), channel_id=1, source_target_pairs={{0,2},{2,0},{1,3},{3,1},{4,6},{6,4},{5,7},{7,5},{8,10},{10,8},{9,1... | collective-permute-start | bytes 3342344 | tf_op jit(solution)/shard_map/ppermute | solution.py:14
  234.5 16.0 %collective-permute-start.2 = (bf16[1088,128]{1,0:T(8,128)(2,1)S(1)}, bf16[1088,128]{1,0:T(8,128)(2,1)S(1)}, u32[]{:S(2)}, u32[]{:S(2)}) collective-permute-start(bf16[1088,128]{1,0:T(8,128)(2,1)S(1)} %fusion.16), channel_id=1, source_target_pairs={{0,2},{2,0},{1,3},{3,1},{4,6},{6,4},{5,7},{7,5},{8,10},{10,8},{9,1... | collective-permute-start | bytes 835592 | tf_op jit(solution)/shard_map/ppermute | solution.py:14
  250.6 28.7 %collective-permute-start.3 = (bf16[1088,256]{1,0:T(8,128)(2,1)S(1)}, bf16[1088,256]{1,0:T(8,128)(2,1)S(1)}, u32[]{:S(2)}, u32[]{:S(2)}) collective-permute-start(bf16[1088,256]{1,0:T(8,128)(2,1)S(1)} %maximum_select_fusion.3), channel_id=1, source_target_pairs={{0,4},{4,0},{1,5},{5,1},{2,6},{6,2},{3,7},{7,3},{8,12},{12,8},{9,1... | collective-permute-start | bytes 1671176 | tf_op jit(solution)/shard_map/ppermute | solution.py:14
  279.6 26.6 %collective-permute-start.4 = (bf16[1088,512]{1,0:T(8,128)(2,1)S(1)}, bf16[1088,512]{1,0:T(8,128)(2,1)}, u32[]{:S(2)}, u32[]{:S(2)}) collective-permute-start(bf16[1088,512]{1,0:T(8,128)(2,1)S(1)} %maximum_select_fusion.2), channel_id=1, source_target_pairs={{0,1},{1,0},{2,3},{3,2},{4,5},{5,4},{6,7},{7,6},{8,9},{9,8},{10,11... | collective-permute-start | bytes 3342344 | tf_op jit(solution)/shard_map/ppermute | solution.py:14
  354.7 1.6 copy-start.4
  358.0 21.3 %collective-permute-start.5 = (bf16[128,3584]{1,0:T(8,128)(2,1)S(1)}, bf16[128,3584]{1,0:T(8,128)(2,1)S(1)}, u32[]{:S(2)}, u32[]{:S(2)}) collective-permute-start(bf16[128,3584]{1,0:T(8,128)(2,1)S(1)} %fusion.1), channel_id=1, source_target_pairs={{32,0},{64,32},{96,64},{128,96},{160,128},{192,160},{224,192},{256... | collective-permute-start | bytes 2752520 | tf_op jit(solution)/shard_map/ppermute | solution.py:20
  364.9 15.6 %collective-permute-start.6 = (bf16[128,3584]{1,0:T(8,128)(2,1)S(1)}, bf16[128,3584]{1,0:T(8,128)(2,1)}, u32[]{:S(2)}, u32[]{:S(2)}) collective-permute-start(bf16[128,3584]{1,0:T(8,128)(2,1)S(1)} %fusion.1), channel_id=1, source_target_pairs={{0,32},{32,64},{64,96},{96,128},{128,160},{160,192},{192,224},{224... | collective-permute-start | bytes 2752520 | tf_op jit(solution)/shard_map/ppermute | solution.py:20
where the time goes:
time: 384 us; the launch traced here: 383 us
  waiting for transfers between devices  235 us (61%)
  starting transfers between devices  73.7 us (19%)
  blocking collectives  42 us (11%)
  matrix products  11.9 us (3%)
  local copies, waits for them, and re-layouts  10.1 us (3%)
  other arithmetic  9.44 us (2%)
    ppermute x5, waiting for transfers between devices, from_partner(): return lax.ppermute(block, axis, route)  175 us
    ppermute x5, starting transfers between devices, from_partner(): return lax.ppermute(block, axis, route)  51.1 us
    all_to_all x1, waiting for transfers between devices, group_expert(): lax.all_to_all(outgoing, 'expert', split_axis=0, concat_axis=0, tiled=True)  50.4 us
    all_to_all x1, blocking collectives, group_expert(): lax.all_to_all(result, 'expert', split_axis=0, concat_axis=0, tiled=True)  42 us
    ppermute x2, starting transfers between devices, from_behind(): return lax.ppermute(x, axis, pairs)  12.1 us
    all_to_all x1, starting transfers between devices, group_expert(): lax.all_to_all(outgoing, 'expert', split_axis=0, concat_axis=0, tiled=True)  10.5 us
    ppermute x2, waiting for transfers between devices, from_behind(): return lax.ppermute(x, axis, pairs)  10.3 us
  transfers between devices with their start and end apart: 8, of which 8 were waited for; matrix products, arithmetic and copies ran while one was open for 0% of the time, Pallas kernels for 0%

commit v1 on v0

v1 whole, which is shorter than its diff:
```python
import functools
import jax
import jax.numpy as jnp
from jax import lax
from jax.experimental import pallas as pl
from jax.experimental.pallas import tpu as pltpu
from jax.sharding import PartitionSpec as P

MESH = pl.DeviceIdType.MESH
BF = jnp.bfloat16
F32 = jnp.float32

D = 3584
TOK = 128
QD = 896
HB = 512
STAGES = 4
ROWS = TOK // STAGES
FOLD = ROWS * 7 // 2
NEEDS = ((0, 1), (0, 1, 2), (1, 2, 3), (2, 3))


def dot(a, b):
    return jnp.dot(a, b, preferred_element_type=F32)


def iota(shape, axis):
    return lax.broadcasted_iota(jnp.int32, shape, axis)


def onehot(cond):
    return jnp.where(cond, 1.0, 0.0).astype(F32)


def kernel(tok, routing, scores, w_gate, w_up, w_down, out,
           rq, xa, bnd, part, psend, relay, near, hid, lhs, lhd, wgu, wd, wdn,
           osend, oback, toks, dests, scos, dmine, smine, oall,
           s_loc, s_w, r_w, s_b, r_b, s_sib, r_sib, s_tok, r_tok, s_p, r_p,
           s_h, r_h, s_o, r_o):
    pipe = lax.axis_index("pipe")
    place = lax.axis_index("expert")
    x, y = place // 8, place % 8
    a, b = y // 2, y % 2
    sig = 1 - 2 * b
    other = pipe + 1 - 2 * (pipe % 2)

    def m8(v):
        return lax.rem(v + 16, 8)

    def on_line(v):
        return (pipe, x * 8 + m8(v))

    def on_cross(v):
        return (pipe, lax.rem(x + v + 4, 4) * 8 + y)

    barrier = pltpu.get_barrier_semaphore()
    for d in range(1, 8):
        pl.semaphore_signal(barrier, inc=1, device_id=on_line(y + d), device_id_type=MESH)
    for d in range(1, 4):
        pl.semaphore_signal(barrier, inc=1, device_id=on_cross(d), device_id_type=MESH)
    for d in range(8):
        pl.semaphore_signal(barrier, inc=1, device_id=(other, x * 8 + d), device_id_type=MESH)

    pending = []

    def remote(src, dst, ssem, rsem, device):
        return pltpu.make_async_remote_copy(
            src_ref=src, dst_ref=dst, send_sem=ssem, recv_sem=rsem,
            device_id=device, device_id_type=MESH)

    def send(*args):
        copy = remote(*args)
        copy.start()
        pending.append(copy)
        return copy

    def sent(copies):
        for copy in copies:
            copy.wait_send()
            pending[:] = [c for c in pending if c is not copy]

    local = []
    for n, (src, dst) in enumerate(
            ((w_gate, wgu.at[0, 0]), (w_up, wgu.at[0, 1]), (w_down, wdn))):
        copy = pltpu.make_async_copy(src, dst, s_loc.at[n])
        copy.start()
        local.append(copy)

    rel = lax.rem(routing[...] - x + 4, 4)
    key = jnp.where(rel == 2, 3, jnp.where(rel == 3, 2, rel))
    lane = iota((TOK, TOK), 1)
    sub = iota((TOK, TOK), 0)
    member = onehot(key == lane)
    member16 = member.astype(BF)
    before = dot(onehot(lane < sub).astype(BF), member16)
    total = dot(jnp.ones((TOK, TOK), BF), member16)
    start = dot(total.astype(BF), onehot(sub < lane).astype(BF))
    dest = jnp.sum((start + before) * member, axis=1, keepdims=True)
    dest = jnp.broadcast_to(dest, (TOK, TOK))
    dmine[...] = dest
    smine[...] = jnp.broadcast_to(scores[...], (TOK, TOK))
    first = jnp.sum(
        jnp.where(lane[:8] == sub[:8], start[:8], 0.0), axis=1, keepdims=True)
    bnd[y] = jnp.broadcast_to(first, (8, TOK))
    place_of = onehot(dest == lane.astype(F32)).T.astype(BF)

    pl.semaphore_wait(barrier, 18)

    def send_w(n, slot):
        src = (w_gate, w_up, wd.at[0])[n]
        dst = (wgu.at[slot, 0], wgu.at[slot, 1], wd.at[slot])[n]
        to = (-1, 1, 2)[slot - 1]
        return send(src, dst, s_w.at[n, slot - 1], r_w.at[n, slot - 1], on_cross(to))

    def wait_w(n, slot):
        dst = (wgu.at[slot, 0], wgu.at[slot, 1], wd.at[slot])[n]
        src = (w_gate, w_up, wd.at[0])[n]
        remote(src, dst, s_w.at[n, slot - 1], r_w.at[n, slot - 1], on_cross(1)).wait_recv()

    first_w = [send_w(n, slot) for n in (0, 1) for slot in (1, 2)]

    kinds = (sig, 2 * sig, -sig, -3 * sig)
    sources = [m8(y + v) for v in
               (sig, -2 * sig, -sig, -3 * sig, 3 * sig, 2 * sig, 4 * sig)]

    for d in range(1, 8):
        send(bnd.at[y], bnd.at[y], s_b.at[d - 1], r_b.at[d - 1], on_line(y + d))

    for i in range(STAGES):
        rows = pl.ds(i * ROWS, ROWS)
        for q in range(4):
            rq[q, rows, :] = dot(
                place_of[i * ROWS:(i + 1) * ROWS], tok[:, q * QD:(q + 1) * QD]).astype(BF)
        for k in (3, 1, 2, 0):
            to = m8(y + kinds[k])
            send(rq.at[to // 2, rows], xa.at[y, rows],
                 s_tok.at[i, k], r_tok.at[i, k], on_line(to))
        xa[y, rows, :] = rq[a, rows, :]

    send(tok, toks, s_sib.at[0], r_sib.at[0], (other, place))
    send(dmine, dests, s_sib.at[1], r_sib.at[1], (other, place))
    send(smine, scos, s_sib.at[2], r_sib.at[2], (other, place))

    def tok_arrived(i, k):
        at = xa.at[sources[k], pl.ds(i * ROWS, ROWS)]
        remote(at, at, s_tok.at[i, k], r_tok.at[i, k], on_line(y + 1)).wait_recv()
        return at

    def forward(i):
        for k in (2, 1, 3):
            at = tok_arrived(i, k)
            send(at, at, s_tok.at[i, k + 3], r_tok.at[i, k + 3], on_line(y + sig))

    def order_down():
        for copy in local:
            copy.wait()
        c = iota((448, 512), 0)
        l = iota((448, 512), 1)
        from_col = jnp.where(l < 384, l + 64 * b, l % 64 + 384 * (1 - b))
        pick = onehot(c == from_col).astype(BF)

        @pl.loop(0, 4)
        def _(r):
            at = pl.ds(pl.multiple_of(r * 256, 256), 256)
            wd[0, at, :] = dot(wdn[at, :], pick).astype(BF)

    def mask(s, i, j):
        row = iota((ROWS, TOK), 0).astype(F32) + float(i * ROWS)
        low = bnd[s, j:j + 1, :]
        high = bnd[s, j + 1:j + 2, :]
        return onehot((row >= low) & (row < high)).astype(BF)

    def partial(i):
        rows = pl.ds(i * ROWS, ROWS)
        for n, j in enumerate(NEEDS[i]):
            @pl.loop(0, 8)
            def _(s):
                m = mask(s, i, j)
                at = pl.ds(pl.multiple_of(s * ROWS, ROWS), ROWS)
                for c in range(7):
                    lanes = pl.ds(c * TOK, TOK)
                    lhs[n, at, lanes] = xa[s, rows, lanes] * m

        @pl.loop(0, 4)
        def _(c):
            at = pl.ds(pl.multiple_of((c % 2) * 256, 256), 256)
            acc = None
            for n, j in enumerate(NEEDS[i]):
                term = dot(lhs[n], wgu[j, c // 2, :, at])
                acc = term if acc is None else acc + term
            acc = acc.reshape(8, ROWS, 256)
            col = pl.ds(pl.multiple_of(c * 256, 256), 256)
            part[:, rows, col] = acc
            psend[:, rows, col] = acc.astype(BF)

    far = 2 * lax.rem(a + 2, 4)
    up = 2 * lax.rem(a + 1, 4)
    down = 2 * lax.rem(a + 3, 4)

    def p_copy(i, k):
        rows = pl.ds(i * ROWS, ROWS)
        src = (far, far + 1, up + 1, down, up, down + 1)[k]
        dst = (relay.at[0, rows], relay.at[1, rows], near.at[0, 1, rows],
               near.at[1, 0, rows], near.at[0, 0, rows], near.at[1, 1, rows])[k]
        to = (2, -2, 2, -2, 2, -2)[k]
        return remote(psend.at[src, rows], dst, s_p.at[i, k], r_p.at[i, k], on_line(y + to))

    def p_start(i, ks):
        for k in ks:
            copy = p_copy(i, k)
            copy.start()
            pending.append(copy)

    def relayed(i):
        rows = pl.ds(i * ROWS, ROWS)
        for k, s in ((0, up), (1, down + 1)):
            p_copy(i, k).wait_recv()
            psend[s, rows, :] = (
                part[s, rows, :] + relay[k, rows, :].astype(F32)).astype(BF)
            p_start(i, (k + 4,))

    def h_copy(i, t, way):
        step = (1, -1)[way]
        owner = m8(y - step * (t - 1))
        rows = pl.ds(i * ROWS, ROWS)
        src = 2 * (owner // 2)
        if t == 4:
            at = hid.at[owner % 2, pl.ds(src + way, 1), rows]
        else:
            at = hid.at[owner % 2, pl.ds(src, 2), rows]
        return remote(at, at, s_h.at[i, t - 1, way], r_h.at[i, t - 1, way], on_line(y + step))

    def h_start(i, t):
        for way in (0, 1):
            copy = h_copy(i, t, way)
            copy.start()
            pending.append(copy)

    def h_arrived(i, t):
        for way in (0, 1):
            step = (1, -1)[way]
            owner = m8(y - step * t)
            rows = pl.ds(i * ROWS, ROWS)
            src = 2 * (owner // 2)
            if t == 4:
                at = hid.at[owner % 2, pl.ds(src + way, 1), rows]
            else:
                at = hid.at[owner % 2, pl.ds(src, 2), rows]
            remote(at, at, s_h.at[i, t - 1, way], r_h.at[i, t - 1, way],
                   on_line(y + step)).wait_recv()

    def hidden(i):
        rows = pl.ds(i * ROWS, ROWS)
        for k in (2, 3, 4, 5):
            p_copy(i, k).wait_recv()
        for k in (0, 1):
            s = 2 * a + k
            whole = (part[s, rows, :] + near[0, k, rows, :].astype(F32)
                     + near[1, k, rows, :].astype(F32))
            g, u = whole[:, :HB], whole[:, HB:]
            hid[b, s, rows, :] = (g / (1.0 + jnp.exp(-g)) * u).astype(BF)
        h_start(i, 1)

    def pass_on(i, t):
        h_arrived(i, t - 1)
        h_start(i, t)

    def expert_out(i):
        h_arrived(i, 4)
        rows = pl.ds(i * ROWS, ROWS)
        for n, j in enumerate(NEEDS[i]):
            @pl.loop(0, 8)
            def _(s):
                m = mask(s, i, j)
                at = pl.ds(pl.multiple_of(s * ROWS, ROWS), ROWS)
                for c in range(8):
                    lhd[n, at, pl.ds(c * TOK, TOK)] = (
                        hid[c // 4, s, rows, pl.ds((c % 4) * TOK, TOK)] * m)

        keep = iota((16, TOK), 1) // 64 == b
        half = ROWS // 2
        base = i * FOLD

        @pl.loop(0, 2)
        def _(c):
            at = pl.ds(pl.multiple_of(c * 256, 256), 256)
            acc = None
            for n, j in enumerate(NEEDS[i]):
                term = dot(lhd[n], wd[j, :, at])
                acc = term if acc is None else acc + term
            acc = acc.reshape(8, ROWS, 256)
            low = base + c * (2 * ROWS)
            osend[:, pl.ds(pl.multiple_of(low, 16), ROWS), :] = acc[:, :, :TOK].astype(BF)

            @pl.when(c == 0)
            def _():
                osend[:, pl.ds(base + ROWS, ROWS), :] = acc[:, :, TOK:].astype(BF)

            @pl.when(c == 1)
            def _():
                folded = jnp.where(keep[None], acc[:, :half, TOK:], acc[:, half:, TOK:])
                osend[:, pl.ds(base + 3 * ROWS, half), :] = folded.astype(BF)

        fold = pl.ds(base, FOLD)
        for d in (4, 3, 5, 2, 6, 1, 7, 0):
            to = m8(y + d)
            send(osend.at[to, fold], oback.at[y, fold],
                 s_o.at[i, d], r_o.at[i, d], (other, x * 8 + to))

    def collect(i):
        base = i * FOLD
        fold = pl.ds(base, FOLD)
        for d in range(8):
            at = oback.at[m8(y - d), fold]
            remote(at, at, s_o.at[i, d], r_o.at[i, d], (other, place)).wait_recv()
        half = ROWS // 2
        low_lanes = iota((half, TOK), 1) < 64
        for m in range(4):
            col = m * QD
            for c in range(3):
                r = pl.ds(base + c * ROWS, ROWS)
                oall[pl.ds(i * ROWS, ROWS), pl.ds(col + c * TOK, TOK)] = oback[2 * m, r, :]
                oall[pl.ds(i * ROWS, ROWS), pl.ds(col + 512 + c * TOK, TOK)] = (
                    oback[2 * m + 1, r, :])
            r = pl.ds(base + 3 * ROWS, half)
            even = oback[2 * m, r, :].astype(F32)
            odd = oback[2 * m + 1, r, :].astype(F32)
            oall[pl.ds(i * ROWS, half), pl.ds(col + 384, TOK)] = (
                jnp.where(low_lanes, even, odd).astype(BF))
            oall[pl.ds(i * ROWS + half, half), pl.ds(col + 384, TOK)] = (
                pltpu.roll(jnp.where(low_lanes, odd, even), 64, 1).astype(BF))

    for i in range(STAGES):
        forward(i)
        if i == 0:
            order_down()
            for d in range(1, 8):
                at = bnd.at[m8(y - d)]
                remote(at, at, s_b.at[d - 1], r_b.at[d - 1], on_line(y + d)).wait_recv()
    for i in range(STAGES):
        for k in (0, 4, 5, 6):
            tok_arrived(i, k)

    sent(first_w)
    last_w = [send_w(n, 3) for n in (0, 1)]
    for n in (0, 1):
        for slot in (1, 2):
            wait_w(n, slot)
    partial(0)
    p_start(0, range(4))
    partial(1)
    p_start(1, range(4))
    relayed(0)
    relayed(1)
    hidden(0)
    pass_on(0, 2)
    pass_on(0, 3)
    hidden(1)
    pass_on(0, 4)
    pass_on(1, 2)
    sent(last_w)
    down_w = [send_w(2, slot) for slot in (1, 2)]
    for n in (0, 1):
        wait_w(n, 3)
    partial(2)
    p_start(2, range(4))
    partial(3)
    p_start(3, range(4))
    pass_on(1, 3)
    pass_on(1, 4)
    relayed(2)
    relayed(3)
    sent(down_w)
    send_w(2, 3)
    hidden(2)
    pass_on(2, 2)
    pass_on(2, 3)
    hidden(3)
    pass_on(2, 4)
    pass_on(3, 2)
    for slot in (1, 2):
        wait_w(2, slot)
    expert_out(0)
    expert_out(1)
    pass_on(3, 3)
    pass_on(3, 4)
    wait_w(2, 3)
    expert_out(2)
    expert_out(3)
    remote(tok, toks, s_sib.at[0], r_sib.at[0], (other, place)).wait_recv()
    remote(dmine, dests, s_sib.at[1], r_sib.at[1], (other, place)).wait_recv()
    remote(smine, scos, s_sib.at[2], r_sib.at[2], (other, place)).wait_recv()
    for i in range(STAGES):
        collect(i)

    back = onehot(dests[...] == lane.astype(F32)).astype(BF)

    @pl.loop(0, 7)
    def _(c):
        at = pl.ds(pl.multiple_of(c * 512, 512), 512)
        gain = scos[...]
        moved = dot(back, oall[:, at])
        gain = jnp.concatenate([gain] * 4, axis=1)
        out[:, at] = (toks[:, at].astype(F32) + gain * moved).astype(BF)

    for copy in pending:
        copy.wait_send()


def body(tokens, routing, scores, w_gate, w_up, w_down):
    vmem = pl.BlockSpec(memory_space=pltpu.VMEM)
    hbm = pl.BlockSpec(memory_space=pl.ANY)
    dma = pltpu.SemaphoreType.DMA
    result = pl.pallas_call(
        kernel,
        out_shape=jax.ShapeDtypeStruct((TOK, D), BF),
        in_specs=[vmem, vmem, vmem, hbm, hbm, hbm],
        out_specs=vmem,
        scratch_shapes=[
            pltpu.VMEM((4, TOK, QD), BF),
            pltpu.VMEM((8, TOK, QD), BF),
            pltpu.VMEM((8, 8, TOK), F32),
            pltpu.VMEM((8, TOK, 2 * HB), F32),
            pltpu.VMEM((8, TOK, 2 * HB), BF),
            pltpu.VMEM((2, TOK, 2 * HB), BF),
            pltpu.VMEM((2, 2, TOK, 2 * HB), BF),
            pltpu.VMEM((2, 8, TOK, HB), BF),
            pltpu.VMEM((3, 8 * ROWS, QD), BF),
            pltpu.VMEM((3, 8 * ROWS, 2 * HB), BF),
            pltpu.VMEM((4, 2, QD, HB), BF),
            pltpu.VMEM((4, 2 * HB, 512), BF),
            pltpu.VMEM((2 * HB, 448), BF),
            pltpu.VMEM((8, STAGES * FOLD, TOK), BF),
            pltpu.VMEM((8, STAGES * FOLD, TOK), BF),
            pltpu.VMEM((TOK, D), BF),
            pltpu.VMEM((TOK, TOK), F32),
            pltpu.VMEM((TOK, TOK), F32),
            pltpu.VMEM((TOK, TOK), F32),
            pltpu.VMEM((TOK, TOK), F32),
            pltpu.VMEM((TOK, D), BF),
            dma((3,)),
            dma((3, 3)), dma((3, 3)),
            dma((7,)), dma((7,)),
            dma((3,)), dma((3,)),
            dma((STAGES, 7)), dma((STAGES, 7)),
            dma((STAGES, 6)), dma((STAGES, 6)),
            dma((STAGES, 4, 2)), dma((STAGES, 4, 2)),
            dma((STAGES, 8)), dma((STAGES, 8)),
        ],
        compiler_params=pltpu.CompilerParams(
            collective_id=0, has_side_effects=True, vmem_limit_bytes=52 * 2**20),
        cost_estimate=pl.CostEstimate(
            flops=8 * 10**9, bytes_accessed=6 * 10**6, transcendentals=131072),
    )(tokens[0], routing[0], scores[0], w_gate[0, 0], w_up[0, 0], w_down[0, 0])
    return result[None]


def solution(mesh):
    return jax.shard_map(
        body,
        mesh=mesh,
        in_specs=(
            P("pipe", "expert", None),
            P("pipe", "expert", None),
            P("pipe", "expert", None),
            P("pipe", "expert", None, None),
            P("pipe", "expert", None, None),
            P("pipe", "expert", None, None),
        ),
        out_specs=P("pipe", "expert", None),
        check_vma=False,
    )
```

time: 384 us -> 226 us (0.59)
  waiting for transfers between devices: 235 us -> 0 us
  Pallas kernels: 0 us -> 221 us
  starting transfers between devices: 73.7 us -> 0 us
  blocking collectives: 42 us -> 0 us
  matrix products: 11.9 us -> 0 us
  other arithmetic: 9.44 us -> 0 us
  local copies, waits for them, and re-layouts: 10.1 us -> 4.68 us
    pallas_call x0 -> x1, Pallas kernels: none -> 221 us  [body(): pl.pallas_call(kernel, out_shape=jax.ShapeDtypeStruct((TOK, D), BF), in_s...]
    ppermute x7 -> x0, waiting for transfers between devices: 185 us -> none  [the longest x5 175 us: from_partner(): return lax.ppermute(block, axis, route)]
    ppermute x7 -> x0, starting transfers between devices: 63.2 us -> none  [the longest x5 51.1 us: from_partner(): return lax.ppermute(block, axis, route)]
    all_to_all x1 -> x0, waiting for transfers between devices: 50.4 us -> none  [group_expert(): lax.all_to_all(outgoing, 'expert', split_axis=0, concat_axis=0, tiled=True)]
    all_to_all x1 -> x0, blocking collectives: 42 us -> none  [group_expert(): lax.all_to_all(result, 'expert', split_axis=0, concat_axis=0, tiled=True)]
    dot_general x5 -> x0, matrix products: 11.9 us -> none  [the longest x1 4.29 us: group_expert(): jnp.dot(hidden, down_w, preferred_element_type=jnp.float32)]
    all_to_all x1 -> x0, starting transfers between devices: 10.5 us -> none  [group_expert(): lax.all_to_all(outgoing, 'expert', split_axis=0, concat_axis=0, tiled=True)]
    add x3 -> x0, other arithmetic: 4.56 us -> none  [the longest x2 3.9 us: group_expert(): current = kept_part + from_partner(sent_part, 'expert', bit_index)]
  transfers between devices with their start and end apart: 8 -> 0, of which waited for: 8 -> 0; matrix products, arithmetic and copies ran while one was open for 0% -> 0% of each run, Pallas kernels for 0% -> 0%
where the time goes in v1:
time: 226 us
  Pallas kernels  221 us (98%)
  local copies, waits for them, and re-layouts  4.68 us (2%)
    pallas_call x1, Pallas kernels, body(): pl.pallas_call(kernel, out_shape=jax.ShapeDtypeStruct((TOK, D), BF), in_s...  221 us

profile of v1, /device:TPU:1, one launch (start us, length us, event | category | flops | bytes accessed | tf_op | source)
XLA Modules:
  0.0 225.7 jit_solution(1237415788589077138)
XLA Ops:
  0.0 0.0 copy-start.1
  0.0 0.7 copy-done.1
  0.7 0.0 copy-start.2
  0.7 0.1 copy.8.routing
  0.8 0.5 copy-done.2
  1.3 0.1 copy.9.scores
  1.4 0.0 copy-start
  1.4 2.3 %copy.7 = bf16[1,1,1024,448]{3,2,1,0:T(8,128)(2,1)} copy(bf16[1,1,1024,448]{2,3,1,0:T(8,128)(2,1)} %param.11) | data formatting | bytes 1835008 | tf_op args[5]
  3.8 0.0 copy-done
  3.8 221.0 %shard_map.64 = bf16[128,3584]{1,0:T(8,128)(2,1)S(1)} custom-call(bf16[128,3584]{1,0:T(8,128)(2,1)S(1)} %bitcast.8, s32[128,1]{1,0:T(8,128)S(1)} %copy.8.routing, f32[128,1]{1,0:T(8,128)S(1)} %copy.9.scores, bf16[896,512]{1,0:T(8,128)(2,1)} %bitcast.12, bf16[896,512]{1,0:T(8,128)(2,1)} %bitcast.13, bf16[1024,448]{1,0:T(8,128)(2,1)} %bitcast.9), custom_call_target="tpu_custom_call" | custom-call | flops 8000000000 | bytes 6000000 | tf_op jit(solution)/shard_map/pallas_call | solution.py:414
  224.8 0.9 copy.11
Async XLA Ops:
  0.0 0.7 copy-start.1
  0.7 0.7 copy-start.2
  1.4 2.3 %copy-start = (bf16[1,128,3584]{2,1,0:T(8,128)(2,1)S(1)}, bf16[1,128,3584]{2,1,0:T(8,128)(2,1)}, u32[]{:S(2)}) copy-start(bf16[1,128,3584]{2,1,0:T(8,128)(2,1)} %param.6) | copy-start | bytes 2752516

commit v2 on v1

--- a/solution.py
+++ b/solution.py
@@ -18,6 +18,18 @@
 ROWS = TOK // STAGES
 FOLD = ROWS * 7 // 2
 NEEDS = ((0, 1), (0, 1, 2), (1, 2, 3), (2, 3))
+ORDER = (
+    ("F", 0), ("D",), ("B",), ("F", 1), ("F", 2), ("W", 0), ("F", 3),
+    ("T", 0), ("T", 1), ("T", 2), ("T", 3), ("W", 1), ("V", 2, (0, 1)),
+    ("P", 0), ("P", 1), ("R", 0), ("R", 1), ("H", 0), ("G", 0, 2),
+    ("H", 1), ("G", 0, 3), ("G", 1, 2),
+    ("X", 0, (2, 3)), ("X", 1, (2, 3)),
+    ("P", 2), ("P", 3), ("G", 0, 4), ("G", 1, 3), ("R", 2), ("G", 1, 4), ("R", 3),
+    ("H", 2), ("G", 2, 2), ("H", 3), ("G", 2, 3), ("G", 3, 2), ("W", 2),
+    ("O", 0), ("G", 2, 4), ("G", 3, 3), ("O", 1), ("G", 3, 4),
+    ("X", 2, (2, 3)), ("O", 2), ("O", 3),
+    ("S",), ("C", 0), ("C", 1), ("C", 2), ("C", 3),
+)
 
 
 def dot(a, b):
@@ -33,7 +45,7 @@
 
 
 def kernel(tok, routing, scores, w_gate, w_up, w_down, out,
-           rq, xa, bnd, part, psend, relay, near, hid, lhs, lhd, wgu, wd, wdn,
+           rq, xa, bnd, part, psend, relay, near, hid, lhs, lhd, wgu, wd,
            osend, oback, toks, dests, scos, dmine, smine, oall,
            s_loc, s_w, r_w, s_b, r_b, s_sib, r_sib, s_tok, r_tok, s_p, r_p,
            s_h, r_h, s_o, r_o):
@@ -74,14 +86,9 @@
         pending.append(copy)
         return copy
 
-    def sent(copies):
-        for copy in copies:
-            copy.wait_send()
-            pending[:] = [c for c in pending if c is not copy]
-
     local = []
     for n, (src, dst) in enumerate(
-            ((w_gate, wgu.at[0, 0]), (w_up, wgu.at[0, 1]), (w_down, wdn))):
+            ((w_gate, wgu.at[0, 0]), (w_up, wgu.at[0, 1]), (w_down, wd.at[0]))):
         copy = pltpu.make_async_copy(src, dst, s_loc.at[n])
         copy.start()
         local.append(copy)
@@ -106,18 +113,27 @@
 
     pl.semaphore_wait(barrier, 18)
 
-    def send_w(n, slot):
-        src = (w_gate, w_up, wd.at[0])[n]
-        dst = (wgu.at[slot, 0], wgu.at[slot, 1], wd.at[slot])[n]
-        to = (-1, 1, 2)[slot - 1]
-        return send(src, dst, s_w.at[n, slot - 1], r_w.at[n, slot - 1], on_cross(to))
-
-    def wait_w(n, slot):
-        dst = (wgu.at[slot, 0], wgu.at[slot, 1], wd.at[slot])[n]
-        src = (w_gate, w_up, wd.at[0])[n]
-        remote(src, dst, s_w.at[n, slot - 1], r_w.at[n, slot - 1], on_cross(1)).wait_recv()
-
-    first_w = [send_w(n, slot) for n in (0, 1) for slot in (1, 2)]
+    def w_copy(n, k):
+        own = (w_gate, w_up, w_down)[n]
+        held = [None] + [(wgu.at[j, 0], wgu.at[j, 1], wd.at[j])[n] for j in (1, 2, 3)]
+        size = (QD // 2, QD // 2, 224)[n]
+        halves = (pl.ds(0, size), pl.ds(size, size))
+        src = (own, own, held[1].at[halves[0]], held[2].at[halves[1]])[k]
+        dst = (held[1], held[2], held[3].at[halves[0]], held[3].at[halves[1]])[k]
+        return remote(src, dst, s_w.at[n, k], r_w.at[n, k], on_cross((-1, 1, -1, 1)[k]))
+
+    def w_start(n, ks):
+        for k in ks:
+            copy = w_copy(n, k)
+            copy.start()
+            pending.append(copy)
+
+    def w_wait(n, ks):
+        for k in ks:
+            w_copy(n, k).wait_recv()
+
+    for n in (0, 1):
+        w_start(n, (0, 1))
 
     kinds = (sig, 2 * sig, -sig, -3 * sig)
     sources = [m8(y + v) for v in
@@ -151,18 +167,9 @@
             at = tok_arrived(i, k)
             send(at, at, s_tok.at[i, k + 3], r_tok.at[i, k + 3], on_line(y + sig))
 
-    def order_down():
+    def own_weights():
         for copy in local:
             copy.wait()
-        c = iota((448, 512), 0)
-        l = iota((448, 512), 1)
-        from_col = jnp.where(l < 384, l + 64 * b, l % 64 + 384 * (1 - b))
-        pick = onehot(c == from_col).astype(BF)
-
-        @pl.loop(0, 4)
-        def _(r):
-            at = pl.ds(pl.multiple_of(r * 256, 256), 256)
-            wd[0, at, :] = dot(wdn[at, :], pick).astype(BF)
 
     def mask(s, i, j):
         row = iota((ROWS, TOK), 0).astype(F32) + float(i * ROWS)
@@ -281,25 +288,25 @@
         half = ROWS // 2
         base = i * FOLD
 
-        @pl.loop(0, 2)
+        def term(n, cols):
+            return lax.dot_general(
+                lhd[n], cols, (((1,), (1,)), ((), ())), preferred_element_type=F32)
+
+        @pl.loop(0, 3)
         def _(c):
-            at = pl.ds(pl.multiple_of(c * 256, 256), 256)
-            acc = None
-            for n, j in enumerate(NEEDS[i]):
-                term = dot(lhd[n], wd[j, :, at])
-                acc = term if acc is None else acc + term
-            acc = acc.reshape(8, ROWS, 256)
-            low = base + c * (2 * ROWS)
-            osend[:, pl.ds(pl.multiple_of(low, 16), ROWS), :] = acc[:, :, :TOK].astype(BF)
-
-            @pl.when(c == 0)
-            def _():
-                osend[:, pl.ds(base + ROWS, ROWS), :] = acc[:, :, TOK:].astype(BF)
-
-            @pl.when(c == 1)
-            def _():
-                folded = jnp.where(keep[None], acc[:, :half, TOK:], acc[:, half:, TOK:])
-                osend[:, pl.ds(base + 3 * ROWS, half), :] = folded.astype(BF)
+            at = pl.ds(pl.multiple_of(c * TOK + 64 * b, 64), TOK)
+            acc = sum(term(n, wd[j, at, :]) for n, j in enumerate(NEEDS[i]))
+            low = pl.multiple_of(base + c * ROWS, 16)
+            osend[:, pl.ds(low, ROWS), :] = acc.reshape(8, ROWS, TOK).astype(BF)
+
+        at = pl.ds(pl.multiple_of(384 * (1 - b), 64), 64)
+        acc = 0.0
+        for n, j in enumerate(NEEDS[i]):
+            rest = wd[j, at, :]
+            acc = acc + term(n, jnp.concatenate([rest, rest], axis=0))
+        acc = acc.reshape(8, ROWS, TOK)
+        folded = jnp.where(keep[None], acc[:, :half], acc[:, half:])
+        osend[:, pl.ds(base + 3 * ROWS, half), :] = folded.astype(BF)
 
         fold = pl.ds(base, FOLD)
         for d in (4, 3, 5, 2, 6, 1, 7, 0):
@@ -330,68 +337,35 @@
             oall[pl.ds(i * ROWS + half, half), pl.ds(col + 384, TOK)] = (
                 pltpu.roll(jnp.where(low_lanes, odd, even), 64, 1).astype(BF))
 
-    for i in range(STAGES):
-        forward(i)
-        if i == 0:
-            order_down()
-            for d in range(1, 8):
-                at = bnd.at[m8(y - d)]
-                remote(at, at, s_b.at[d - 1], r_b.at[d - 1], on_line(y + d)).wait_recv()
-    for i in range(STAGES):
+    def bounds():
+        for d in range(1, 8):
+            at = bnd.at[m8(y - d)]
+            remote(at, at, s_b.at[d - 1], r_b.at[d - 1], on_line(y + d)).wait_recv()
+
+    def tokens_in(i):
         for k in (0, 4, 5, 6):
             tok_arrived(i, k)
 
-    sent(first_w)
-    last_w = [send_w(n, 3) for n in (0, 1)]
-    for n in (0, 1):
-        for slot in (1, 2):
-            wait_w(n, slot)
-    partial(0)
-    p_start(0, range(4))
-    partial(1)
-    p_start(1, range(4))
-    relayed(0)
-    relayed(1)
-    hidden(0)
-    pass_on(0, 2)
-    pass_on(0, 3)
-    hidden(1)
-    pass_on(0, 4)
-    pass_on(1, 2)
-    sent(last_w)
-    down_w = [send_w(2, slot) for slot in (1, 2)]
-    for n in (0, 1):
-        wait_w(n, 3)
-    partial(2)
-    p_start(2, range(4))
-    partial(3)
-    p_start(3, range(4))
-    pass_on(1, 3)
-    pass_on(1, 4)
-    relayed(2)
-    relayed(3)
-    sent(down_w)
-    send_w(2, 3)
-    hidden(2)
-    pass_on(2, 2)
-    pass_on(2, 3)
-    hidden(3)
-    pass_on(2, 4)
-    pass_on(3, 2)
-    for slot in (1, 2):
-        wait_w(2, slot)
-    expert_out(0)
-    expert_out(1)
-    pass_on(3, 3)
-    pass_on(3, 4)
-    wait_w(2, 3)
-    expert_out(2)
-    expert_out(3)
-    remote(tok, toks, s_sib.at[0], r_sib.at[0], (other, place)).wait_recv()
-    remote(dmine, dests, s_sib.at[1], r_sib.at[1], (other, place)).wait_recv()
-    remote(smine, scos, s_sib.at[2], r_sib.at[2], (other, place)).wait_recv()
-    for i in range(STAGES):
-        collect(i)
+    def partial_out(i):
+        partial(i)
+        p_start(i, range(4))
+
+    def pass_weights(n):
+        for k in (0, 1):
+            w_wait(n, (k,))
+            w_start(n, (k + 2,))
+
+    def from_other_core():
+        remote(tok, toks, s_sib.at[0], r_sib.at[0], (other, place)).wait_recv()
+        remote(dmine, dests, s_sib.at[1], r_sib.at[1], (other, place)).wait_recv()
+        remote(smine, scos, s_sib.at[2], r_sib.at[2], (other, place)).wait_recv()
+
+    work = dict(
+        F=forward, D=own_weights, B=bounds, T=tokens_in, W=pass_weights, V=w_start,
+        X=w_wait, P=partial_out, R=relayed, H=hidden, G=pass_on, O=expert_out,
+        S=from_other_core, C=collect)
+    for step in ORDER:
+        work[step[0]](*step[1:])
 
     back = onehot(dests[...] == lane.astype(F32)).astype(BF)
 
@@ -428,8 +402,7 @@
             pltpu.VMEM((3, 8 * ROWS, QD), BF),
             pltpu.VMEM((3, 8 * ROWS, 2 * HB), BF),
             pltpu.VMEM((4, 2, QD, HB), BF),
-            pltpu.VMEM((4, 2 * HB, 512), BF),
-            pltpu.VMEM((2 * HB, 448), BF),
+            pltpu.VMEM((4, 448, 2 * HB), BF),
             pltpu.VMEM((8, STAGES * FOLD, TOK), BF),
             pltpu.VMEM((8, STAGES * FOLD, TOK), BF),
             pltpu.VMEM((TOK, D), BF),
@@ -439,7 +412,7 @@
             pltpu.VMEM((TOK, TOK), F32),
             pltpu.VMEM((TOK, D), BF),
             dma((3,)),
-            dma((3, 3)), dma((3, 3)),
+            dma((3, 4)), dma((3, 4)),
             dma((7,)), dma((7,)),
             dma((3,)), dma((3,)),
             dma((STAGES, 7)), dma((STAGES, 7)),
@@ -451,7 +424,7 @@
             collective_id=0, has_side_effects=True, vmem_limit_bytes=52 * 2**20),
         cost_estimate=pl.CostEstimate(
             flops=8 * 10**9, bytes_accessed=6 * 10**6, transcendentals=131072),
-    )(tokens[0], routing[0], scores[0], w_gate[0, 0], w_up[0, 0], w_down[0, 0])
+    )(tokens[0], routing[0], scores[0], w_gate[0, 0], w_up[0, 0], w_down[0, 0].T)
     return result[None]
 
 

time: 226 us -> 149 us (0.66)
  the two profiles are of different devices: /device:TPU:1 before, /device:TPU:7 now
where the time goes in v2:
time: 149 us
  Pallas kernels  145 us (97%)
  local copies, waits for them, and re-layouts  3.52 us (2%)
    pallas_call x1, Pallas kernels, body(): pl.pallas_call(kernel, out_shape=jax.ShapeDtypeStruct((TOK, D), BF), in_s...  145 us
    unnamed x7, local copies, waits for them, and re-layouts  3.3 us

profile of v2, /device:TPU:7, one launch (start us, length us, event | category | flops | bytes accessed | tf_op | source)
XLA Modules:
  0.0 148.9 jit_solution(1479830665958322875)
XLA Ops:
  0.0 0.0 copy-start.1
  0.0 0.7 copy-done.1
  0.7 0.0 copy-start.2
  0.7 0.1 copy.7.routing
  0.8 0.5 copy-done.2
  1.3 0.1 copy.8.scores
  1.4 0.0 copy-start
  1.4 1.2 copy-done
  2.6 145.4 %shard_map.64 = bf16[128,3584]{1,0:T(8,128)(2,1)S(1)} custom-call(bf16[128,3584]{1,0:T(8,128)(2,1)S(1)} %bitcast.10, s32[128,1]{1,0:T(8,128)S(1)} %copy.7.routing, f32[128,1]{1,0:T(8,128)S(1)} %copy.8.scores, bf16[896,512]{1,0:T(8,128)(2,1)} %bitcast.13, bf16[896,512]{1,0:T(8,128)(2,1)} %bitcast.14, bf16[448,1024]{1,0:T(8,128)(2,1)} %bitcast.15), custom_call_target="tpu_custom_call" | custom-call | flops 8000000000 | bytes 6000000 | tf_op jit(solution)/shard_map/pallas_call | solution.py:388
  148.0 0.9 copy.10
Async XLA Ops:
  0.0 0.7 copy-start.1
  0.7 0.7 copy-start.2
  1.4 1.2 copy-start

commit v3 on v2

--- a/solution.py
+++ b/solution.py
@@ -19,15 +19,17 @@
 FOLD = ROWS * 7 // 2
 NEEDS = ((0, 1), (0, 1, 2), (1, 2, 3), (2, 3))
 ORDER = (
-    ("F", 0), ("D",), ("B",), ("F", 1), ("F", 2), ("W", 0), ("F", 3),
-    ("T", 0), ("T", 1), ("T", 2), ("T", 3), ("W", 1), ("V", 2, (0, 1)),
-    ("P", 0), ("P", 1), ("R", 0), ("R", 1), ("H", 0), ("G", 0, 2),
-    ("H", 1), ("G", 0, 3), ("G", 1, 2),
-    ("X", 0, (2, 3)), ("X", 1, (2, 3)),
-    ("P", 2), ("P", 3), ("G", 0, 4), ("G", 1, 3), ("R", 2), ("G", 1, 4), ("R", 3),
-    ("H", 2), ("G", 2, 2), ("H", 3), ("G", 2, 3), ("G", 3, 2), ("W", 2),
+    ("F", 0), ("D",), ("B",), ("F", 1), ("F", 2), ("W", 0), ("W", 1), ("F", 3),
+    ("T", 0), ("T", 1), ("P", 0, 0), ("T", 2), ("P", 1, 0), ("T", 3),
+    ("W", 2), ("W", 3), ("V", 4, (0, 1)),
+    ("P", 0, 1), ("R", 0, 0), ("P", 1, 1), ("R", 1, 0), ("R", 0, 1),
+    ("X", 0, (2, 3)), ("X", 1, (2, 3)), ("P", 2, 0), ("R", 1, 1),
+    ("P", 3, 0), ("H", 0), ("G", 0, 2), ("R", 2, 0), ("H", 1), ("G", 0, 3), ("G", 1, 2),
+    ("X", 2, (2, 3)), ("X", 3, (2, 3)), ("P", 2, 1), ("R", 3, 0), ("P", 3, 1),
+    ("G", 0, 4), ("G", 1, 3), ("R", 2, 1), ("G", 1, 4), ("R", 3, 1),
+    ("H", 2), ("G", 2, 2), ("H", 3), ("G", 2, 3), ("G", 3, 2), ("W", 4),
     ("O", 0), ("G", 2, 4), ("G", 3, 3), ("O", 1), ("G", 3, 4),
-    ("X", 2, (2, 3)), ("O", 2), ("O", 3),
+    ("X", 4, (2, 3)), ("O", 2), ("O", 3),
     ("S",), ("C", 0), ("C", 1), ("C", 2), ("C", 3),
 )
 
@@ -86,10 +88,17 @@
         pending.append(copy)
         return copy
 
+    def w_own(n):
+        if n == 4:
+            return w_down
+        return (w_gate, w_up)[n % 2].at[:, pl.ds(n // 2 * 256, 256)]
+
+    def w_held(n, slot):
+        return wd.at[slot] if n == 4 else wgu.at[slot, n // 2, n % 2]
+
     local = []
-    for n, (src, dst) in enumerate(
-            ((w_gate, wgu.at[0, 0]), (w_up, wgu.at[0, 1]), (w_down, wd.at[0]))):
-        copy = pltpu.make_async_copy(src, dst, s_loc.at[n])
+    for n in range(5):
+        copy = pltpu.make_async_copy(w_own(n), w_held(n, 0), s_loc.at[n])
         copy.start()
         local.append(copy)
 
@@ -114,9 +123,9 @@
     pl.semaphore_wait(barrier, 18)
 
     def w_copy(n, k):
-        own = (w_gate, w_up, w_down)[n]
-        held = [None] + [(wgu.at[j, 0], wgu.at[j, 1], wd.at[j])[n] for j in (1, 2, 3)]
-        size = (QD // 2, QD // 2, 224)[n]
+        own = w_own(n)
+        held = [None] + [w_held(n, slot) for slot in (1, 2, 3)]
+        size = 224 if n == 4 else QD // 2
         halves = (pl.ds(0, size), pl.ds(size, size))
         src = (own, own, held[1].at[halves[0]], held[2].at[halves[1]])[k]
         dst = (held[1], held[2], held[3].at[halves[0]], held[3].at[halves[1]])[k]
@@ -132,7 +141,7 @@
         for k in ks:
             w_copy(n, k).wait_recv()
 
-    for n in (0, 1):
+    for n in range(4):
         w_start(n, (0, 1))
 
     kinds = (sig, 2 * sig, -sig, -3 * sig)
@@ -177,7 +186,7 @@
         high = bnd[s, j + 1:j + 2, :]
         return onehot((row >= low) & (row < high)).astype(BF)
 
-    def partial(i):
+    def masked_tokens(i):
         rows = pl.ds(i * ROWS, ROWS)
         for n, j in enumerate(NEEDS[i]):
             @pl.loop(0, 8)
@@ -186,17 +195,16 @@
                 at = pl.ds(pl.multiple_of(s * ROWS, ROWS), ROWS)
                 for c in range(7):
                     lanes = pl.ds(c * TOK, TOK)
-                    lhs[n, at, lanes] = xa[s, rows, lanes] * m
-
-        @pl.loop(0, 4)
-        def _(c):
-            at = pl.ds(pl.multiple_of((c % 2) * 256, 256), 256)
-            acc = None
-            for n, j in enumerate(NEEDS[i]):
-                term = dot(lhs[n], wgu[j, c // 2, :, at])
-                acc = term if acc is None else acc + term
+                    lhs[i, n, at, lanes] = xa[s, rows, lanes] * m
+
+    def partial(i, c):
+        rows = pl.ds(i * ROWS, ROWS)
+
+        @pl.loop(0, 2)
+        def _(h):
+            acc = sum(dot(lhs[i, n], wgu[j, c, h]) for n, j in enumerate(NEEDS[i]))
             acc = acc.reshape(8, ROWS, 256)
-            col = pl.ds(pl.multiple_of(c * 256, 256), 256)
+            col = pl.ds(pl.multiple_of(c * HB + h * 256, 256), 256)
             part[:, rows, col] = acc
             psend[:, rows, col] = acc.astype(BF)
 
@@ -204,27 +212,31 @@
     up = 2 * lax.rem(a + 1, 4)
     down = 2 * lax.rem(a + 3, 4)
 
-    def p_copy(i, k):
-        rows = pl.ds(i * ROWS, ROWS)
+    def p_copy(i, c, k):
+        rows = pl.ds(i * ROWS, ROWS)
+        cols = pl.ds(c * HB, HB)
         src = (far, far + 1, up + 1, down, up, down + 1)[k]
-        dst = (relay.at[0, rows], relay.at[1, rows], near.at[0, 1, rows],
-               near.at[1, 0, rows], near.at[0, 0, rows], near.at[1, 1, rows])[k]
+        dst = (relay.at[0, rows, cols], relay.at[1, rows, cols],
+               near.at[0, 1, rows, cols], near.at[1, 0, rows, cols],
+               near.at[0, 0, rows, cols], near.at[1, 1, rows, cols])[k]
         to = (2, -2, 2, -2, 2, -2)[k]
-        return remote(psend.at[src, rows], dst, s_p.at[i, k], r_p.at[i, k], on_line(y + to))
-
-    def p_start(i, ks):
+        return remote(psend.at[src, rows, cols], dst, s_p.at[i, c, k], r_p.at[i, c, k],
+                      on_line(y + to))
+
+    def p_start(i, c, ks):
         for k in ks:
-            copy = p_copy(i, k)
+            copy = p_copy(i, c, k)
             copy.start()
             pending.append(copy)
 
-    def relayed(i):
-        rows = pl.ds(i * ROWS, ROWS)
+    def relayed(i, c):
+        rows = pl.ds(i * ROWS, ROWS)
+        cols = pl.ds(c * HB, HB)
         for k, s in ((0, up), (1, down + 1)):
-            p_copy(i, k).wait_recv()
-            psend[s, rows, :] = (
-                part[s, rows, :] + relay[k, rows, :].astype(F32)).astype(BF)
-            p_start(i, (k + 4,))
+            p_copy(i, c, k).wait_recv()
+            psend[s, rows, cols] = (
+                part[s, rows, cols] + relay[k, rows, cols].astype(F32)).astype(BF)
+            p_start(i, c, (k + 4,))
 
     def h_copy(i, t, way):
         step = (1, -1)[way]
@@ -258,14 +270,18 @@
 
     def hidden(i):
         rows = pl.ds(i * ROWS, ROWS)
-        for k in (2, 3, 4, 5):
-            p_copy(i, k).wait_recv()
-        for k in (0, 1):
-            s = 2 * a + k
-            whole = (part[s, rows, :] + near[0, k, rows, :].astype(F32)
-                     + near[1, k, rows, :].astype(F32))
-            g, u = whole[:, :HB], whole[:, HB:]
-            hid[b, s, rows, :] = (g / (1.0 + jnp.exp(-g)) * u).astype(BF)
+        for c in (0, 1):
+            for k in (2, 3, 4, 5):
+                p_copy(i, c, k).wait_recv()
+        for c in (0, 1):
+            cols = pl.ds(c * HB, HB)
+            for k in (0, 1):
+                s = 2 * a + k
+                whole = (part[s, rows, cols] + near[0, k, rows, cols].astype(F32)
+                         + near[1, k, rows, cols].astype(F32))
+                g, u = whole[:, :256], whole[:, 256:]
+                hid[b, s, rows, pl.ds(c * 256, 256)] = (
+                    g / (1.0 + jnp.exp(-g)) * u).astype(BF)
         h_start(i, 1)
 
     def pass_on(i, t):
@@ -346,9 +362,11 @@
         for k in (0, 4, 5, 6):
             tok_arrived(i, k)
 
-    def partial_out(i):
-        partial(i)
-        p_start(i, range(4))
+    def partial_out(i, c):
+        if c == 0:
+            masked_tokens(i)
+        partial(i, c)
+        p_start(i, c, range(4))
 
     def pass_weights(n):
         for k in (0, 1):
@@ -399,9 +417,9 @@
             pltpu.VMEM((2, TOK, 2 * HB), BF),
             pltpu.VMEM((2, 2, TOK, 2 * HB), BF),
             pltpu.VMEM((2, 8, TOK, HB), BF),
-            pltpu.VMEM((3, 8 * ROWS, QD), BF),
+            pltpu.VMEM((STAGES, 3, 8 * ROWS, QD), BF),
             pltpu.VMEM((3, 8 * ROWS, 2 * HB), BF),
-            pltpu.VMEM((4, 2, QD, HB), BF),
+            pltpu.VMEM((4, 2, 2, QD, 256), BF),
             pltpu.VMEM((4, 448, 2 * HB), BF),
             pltpu.VMEM((8, STAGES * FOLD, TOK), BF),
             pltpu.VMEM((8, STAGES * FOLD, TOK), BF),
@@ -411,12 +429,12 @@
             pltpu.VMEM((TOK, TOK), F32),
             pltpu.VMEM((TOK, TOK), F32),
             pltpu.VMEM((TOK, D), BF),
-            dma((3,)),
-            dma((3, 4)), dma((3, 4)),
+            dma((5,)),
+            dma((5, 4)), dma((5, 4)),
             dma((7,)), dma((7,)),
             dma((3,)), dma((3,)),
             dma((STAGES, 7)), dma((STAGES, 7)),
-            dma((STAGES, 6)), dma((STAGES, 6)),
+            dma((STAGES, 2, 6)), dma((STAGES, 2, 6)),
             dma((STAGES, 4, 2)), dma((STAGES, 4, 2)),
             dma((STAGES, 8)), dma((STAGES, 8)),
         ],

time: 149 us -> 141 us (0.946)
  the two profiles are of different devices: /device:TPU:7 before, /device:TPU:1 now
where the time goes in v3:
time: 141 us; the launch traced here: 139 us
  Pallas kernels  136 us (96%)
  local copies, waits for them, and re-layouts  3.52 us (2%)
    pallas_call x1, Pallas kernels, body(): pl.pallas_call(kernel, out_shape=jax.ShapeDtypeStruct((TOK, D), BF), in_s...  136 us
    unnamed x7, local copies, waits for them, and re-layouts  3.3 us

profile of v3, /device:TPU:1, one launch (start us, length us, event | category | flops | bytes accessed | tf_op | source)
XLA Modules:
  0.0 139.0 jit_solution(16783628668732055426)
XLA Ops:
  0.0 0.0 copy-start.1
  0.0 0.7 copy-done.1
  0.7 0.0 copy-start.2
  0.7 0.1 copy.7.routing
  0.8 0.5 copy-done.2
  1.3 0.1 copy.8.scores
  1.4 0.0 copy-start
  1.4 1.2 copy-done
  2.6 135.5 %shard_map.64 = bf16[128,3584]{1,0:T(8,128)(2,1)S(1)} custom-call(bf16[128,3584]{1,0:T(8,128)(2,1)S(1)} %bitcast.10, s32[128,1]{1,0:T(8,128)S(1)} %copy.7.routing, f32[128,1]{1,0:T(8,128)S(1)} %copy.8.scores, bf16[896,512]{1,0:T(8,128)(2,1)} %bitcast.13, bf16[896,512]{1,0:T(8,128)(2,1)} %bitcast.14, bf16[448,1024]{1,0:T(8,128)(2,1)} %bitcast.15), custom_call_target="tpu_custom_call" | custom-call | flops 8000000000 | bytes 6000000 | tf_op jit(solution)/shard_map/pallas_call | solution.py:406
  138.1 0.9 copy.10
Async XLA Ops:
  0.0 0.7 copy-start.1
  0.7 0.7 copy-start.2
  1.4 1.2 copy-start

commit v4 on v3

--- a/solution.py
+++ b/solution.py
@@ -19,18 +19,15 @@
 FOLD = ROWS * 7 // 2
 NEEDS = ((0, 1), (0, 1, 2), (1, 2, 3), (2, 3))
 ORDER = (
-    ("F", 0), ("D",), ("B",), ("F", 1), ("F", 2), ("W", 0), ("W", 1), ("F", 3),
-    ("T", 0), ("T", 1), ("P", 0, 0), ("T", 2), ("P", 1, 0), ("T", 3),
-    ("W", 2), ("W", 3), ("V", 4, (0, 1)),
-    ("P", 0, 1), ("R", 0, 0), ("P", 1, 1), ("R", 1, 0), ("R", 0, 1),
-    ("X", 0, (2, 3)), ("X", 1, (2, 3)), ("P", 2, 0), ("R", 1, 1),
-    ("P", 3, 0), ("H", 0), ("G", 0, 2), ("R", 2, 0), ("H", 1), ("G", 0, 3), ("G", 1, 2),
-    ("X", 2, (2, 3)), ("X", 3, (2, 3)), ("P", 2, 1), ("R", 3, 0), ("P", 3, 1),
-    ("G", 0, 4), ("G", 1, 3), ("R", 2, 1), ("G", 1, 4), ("R", 3, 1),
-    ("H", 2), ("G", 2, 2), ("H", 3), ("G", 2, 3), ("G", 3, 2), ("W", 4),
-    ("O", 0), ("G", 2, 4), ("G", 3, 3), ("O", 1), ("G", 3, 4),
-    ("X", 4, (2, 3)), ("O", 2), ("O", 3),
-    ("S",), ("C", 0), ("C", 1), ("C", 2), ("C", 3),
+    ("F", 0), ("D",), ("B",), ("F", 1), ("F", 2), ("W", 0), ("W", 1), ("F", 3), ("T", 0),
+    ("T", 1), ("P", 0, 0), ("T", 2), ("P", 1, 0), ("T", 3), ("W", 2), ("W", 3),
+    ("V", 4, (0, 1)), ("P", 0, 1), ("R", 0, 0), ("P", 1, 1), ("R", 1, 0), ("R", 0, 1),
+    ("X", 0, (2, 3)), ("X", 1, (2, 3)), ("P", 2, 0), ("R", 1, 1), ("P", 3, 0), ("H", 0),
+    ("G", 0, 2), ("R", 2, 0), ("H", 1), ("G", 0, 3), ("G", 1, 2), ("X", 2, (2, 3)),
+    ("X", 3, (2, 3)), ("P", 2, 1), ("R", 3, 0), ("P", 3, 1), ("G", 0, 4), ("G", 1, 3),
+    ("R", 2, 1), ("G", 1, 4), ("R", 3, 1), ("H", 2), ("G", 2, 2), ("H", 3), ("G", 2, 3),
+    ("G", 3, 2), ("W", 4), ("O", 0), ("O", 1), ("G", 3, 3), ("G", 2, 4), ("X", 4, (2, 3)),
+    ("G", 3, 4), ("O", 2), ("O", 3), ("S",), ("C", 0), ("C", 1), ("C", 2), ("C", 3),
 )
 
 

time: 141 us -> 139 us (0.986)
  Pallas kernels: 136 us -> 134 us
    pallas_call x1, Pallas kernels: 136 us -> 134 us  [body(): pl.pallas_call(kernel, out_shape=jax.ShapeDtypeStruct((TOK, D), BF), in_s...]
where the time goes in v4:
time: 139 us; the launch traced here: 137 us
  Pallas kernels  134 us (96%)
  local copies, waits for them, and re-layouts  3.52 us (3%)
    pallas_call x1, Pallas kernels, body(): pl.pallas_call(kernel, out_shape=jax.ShapeDtypeStruct((TOK, D), BF), in_s...  134 us
    unnamed x7, local copies, waits for them, and re-layouts  3.3 us

profile of v4, /device:TPU:1, one launch (start us, length us, event | category | flops | bytes accessed | tf_op | source)
XLA Modules:
  0.0 137.1 jit_solution(3159692161092331205)
XLA Ops:
  0.0 0.0 copy-start.1
  0.0 0.7 copy-done.1
  0.7 0.0 copy-start.2
  0.7 0.1 copy.7.routing
  0.8 0.5 copy-done.2
  1.3 0.1 copy.8.scores
  1.4 0.0 copy-start
  1.4 1.2 copy-done
  2.6 133.6 %shard_map.64 = bf16[128,3584]{1,0:T(8,128)(2,1)S(1)} custom-call(bf16[128,3584]{1,0:T(8,128)(2,1)S(1)} %bitcast.10, s32[128,1]{1,0:T(8,128)S(1)} %copy.7.routing, f32[128,1]{1,0:T(8,128)S(1)} %copy.8.scores, bf16[896,512]{1,0:T(8,128)(2,1)} %bitcast.13, bf16[896,512]{1,0:T(8,128)(2,1)} %bitcast.14, bf16[448,1024]{1,0:T(8,128)(2,1)} %bitcast.15), custom_call_target="tpu_custom_call" | custom-call | flops 8000000000 | bytes 6000000 | tf_op jit(solution)/shard_map/pallas_call | solution.py:403
  136.2 0.9 copy.10
Async XLA Ops:
  0.0 0.7 copy-start.1
  0.7 0.7 copy-start.2
  1.4 1.2 copy-start
